TPU v7x, 32 devices: a whole 2x2x4 slice. The times are simulated.
32 devices in a mesh: grp: 2 (over y), ctx: 8 (over z, x), tp: 2 (over core).
Axes of the slice: x: 2, y: 2, z: 4, core: 2. Of those that a mesh axis runs over, the one named last changes fastest.
Arguments:
- queries: bfloat16 [2048, 4096], P(('grp', 'ctx'), 'tp'), parts along dimension 0, may hold values from -6 to 6
- key_proj: bfloat16 [2048, 4096], P(('grp', 'ctx'), 'tp'), parts along dimension 0, may hold values from -6 to 6
- value_proj: bfloat16 [2048, 4096], P(('grp', 'ctx'), 'tp'), parts along dimension 0, may hold values from -6 to 6
- out_grad: bfloat16 [2048, 4096], P(('grp', 'ctx', 'tp')), parts along dimension 0, may hold values from -23 to 23
- filter_taps: bfloat16 [128, 4096], P(None, 'tp'), may hold values from -0.5 to 0.5
Outputs:
- query_grad: bfloat16 [2048, 4096], P(('grp', 'ctx'), 'tp'), parts along dimension 0
- key_grad: bfloat16 [2048, 4096], P(('grp', 'ctx'), 'tp'), parts along dimension 0
- value_grad: bfloat16 [2048, 4096], P(('grp', 'ctx'), 'tp'), parts along dimension 0
- filter_grad: bfloat16 [128, 8192], P(None, ('grp', 'tp')), parts along dimension 1
There are 2 independent parts, one for each index of `grp`. A program takes and returns all parts, laid end to end along the dimension named above; an argument that names none is the same for every part. Nothing has to cross between parts.
All inputs are finite; a program needn't handle non-finite values.
Results may differ from a plain program's by a relative error of at most 0.0057.
Values may be sent and summed in bfloat16 or wider, within the bound.
A program may use at most 64 MiB of HBM per device.

v0:
```python
import math

import jax
import jax.numpy as jnp
from jax import lax
from jax.sharding import PartitionSpec as P


def extended_2(array, sides, width):
    for axis, dim in sides:
        peers, length = (lax.axis_size(axis), array.shape[dim])
        up = [(i, (i + 1) % peers) for i in range(peers - 1)]
        down = [(j, i) for i, j in up]
        last = lax.slice_in_dim(array, length - width, length, axis=dim)
        leading = lax.slice_in_dim(array, 0, width, axis=dim)
        before = lax.ppermute(last, axis, up)
        after = lax.ppermute(leading, axis, down)
        array = jnp.concatenate([before, array, after], axis=dim)
    return array


def forward_sweep(padded, gated, weights, tok_rows, margin):
    channels = padded.shape[1]
    groups = weights.shape[0] // 16

    def forward_stepper(number, carry):
        mixture, tap_rows = carry
        window = lax.dynamic_slice_in_dim(padded, margin - 16 * number - 15, tok_rows + 15, 0)
        coeffs = lax.dynamic_slice_in_dim(weights, 16 * number, 16, 0)
        sums_list = []
        for within in range(16):
            shifted = window[15 - within : 15 - within + tok_rows].astype(jnp.float32)
            mixture = mixture + coeffs[within] * shifted
            sums_list.append(jnp.sum(gated.astype(jnp.float32) * shifted, axis=0))
        tap_rows = lax.dynamic_update_slice_in_dim(tap_rows, jnp.stack(sums_list), 16 * number, 0)
        return (mixture, tap_rows)

    initial = (jnp.zeros((tok_rows, channels), jnp.float32), jnp.zeros(weights.shape, jnp.float32))
    return lax.fori_loop(0, groups, forward_stepper, initial)


def backward_sweep(padded, weights, tok_rows):
    channels = padded.shape[1]
    groups = weights.shape[0] // 16

    def backward_stepper(number, spread):
        window = lax.dynamic_slice_in_dim(padded, 16 * number, tok_rows + 15, 0)
        coeffs = lax.dynamic_slice_in_dim(weights, 16 * number, 16, 0)
        for within in range(16):
            spread = spread + coeffs[within] * window[within : within + tok_rows].astype(
                jnp.float32
            )
        return spread

    return lax.fori_loop(0, groups, backward_stepper, jnp.zeros((tok_rows, channels), jnp.float32))


def local(queries, key_proj, value_proj, out_grad, filter_taps):
    tok_rows = queries.shape[0]
    channels = queries.shape[1]
    margin = filter_taps.shape[0] - 1
    gathered = lax.all_gather(out_grad, "tp", axis=0, tiled=True)
    upstream = lax.dynamic_slice_in_dim(gathered, lax.axis_index("tp") * channels, channels, 1)
    product = (key_proj.astype(jnp.float32) * value_proj).astype(jnp.bfloat16)
    gated = (upstream.astype(jnp.float32) * queries).astype(jnp.bfloat16)
    stacked = jnp.stack([product, gated])
    extended = extended_2(stacked, (("ctx", 1),), margin)
    kv_padded = extended[0, : tok_rows + margin]
    gate_padded = extended[1, margin:]
    weights = filter_taps.astype(jnp.float32)
    mixture, tap_rows = forward_sweep(kv_padded, gated, weights, tok_rows, margin)
    query_grad = (upstream.astype(jnp.float32) * mixture).astype(jnp.bfloat16)
    spread = backward_sweep(gate_padded, weights, tok_rows)
    key_grad = (spread * value_proj).astype(jnp.bfloat16)
    value_grad = (spread * key_proj).astype(jnp.bfloat16)
    scale = 1.0 / math.sqrt(lax.axis_size("ctx") * tok_rows)
    totals = lax.psum(tap_rows, "ctx")
    filter_grad = (totals * scale).astype(jnp.bfloat16)
    return (query_grad, key_grad, value_grad, filter_grad)


def solution(mesh):
    return jax.shard_map(
        local,
        mesh=mesh,
        in_specs=(
            P(("grp", "ctx"), "tp"),
            P(("grp", "ctx"), "tp"),
            P(("grp", "ctx"), "tp"),
            P(("grp", "ctx", "tp"), None),
            P(None, "tp"),
        ),
        out_specs=(
            P(("grp", "ctx"), "tp"),
            P(("grp", "ctx"), "tp"),
            P(("grp", "ctx"), "tp"),
            P(None, ("grp", "tp")),
        ),
        check_vma=False,
    )
```

profile of v0, /device:TPU:0, one launch (start us, length us, event | category | flops | bytes accessed | tf_op | source)
XLA Modules:
  0.0 264.8 jit_solution(6643384166794470438)
XLA Ops:
  7.2 0.7 all-gather.2.cloned.1.call-update
  8.0 1.3 fusion.54
  9.3 12.0 %all-gather.2.cloned.1.call-done = bf16[128,4096]{1,0:T(8,128)(2,1)} async-done(((bf16[64,4096]{1,0:T(8,128)(2,1)}), bf16[128,4096]{1,0:T(8,128)(2,1)}) %all-gather.2.cloned.1.call-update) | async-done | bytes 1048592 | tf_op jit(solution)/shard_map/all_gather | solution.py:62
  21.3 1.2 fusion.47
  23.3 1.1 copy.11
  24.4 1.3 collective-permute-start.1
  25.7 2.0 copy.9
  27.7 5.5 %collective-permute-start = (bf16[2,127,2048]{2,0,1:T(2,128)(2,1)}, bf16[2,127,2048]{2,0,1:T(2,128)(2,1)}, u32[]{:S(2)}, u32[]{:S(2)}) collective-permute-start(bf16[2,127,2048]{2,0,1:T(2,128)(2,1)} %copy.9), channel_id=1, source_target_pairs={{0,2},{2,4},{4,6},{6,8},{8,10},{10,12},{12,14},{1,3},{3,5},{5,7},{... | collective-permute-start | bytes 3121160 | tf_op jit(solution)/shard_map/ppermute | solution.py:16
  33.2 2.2 convert_element_type.385
  35.4 16.0 %collective-permute-done.1 = bf16[2,127,2048]{2,0,1:T(2,128)(2,1)S(1)} collective-permute-done((bf16[2,127,2048]{2,0,1:T(2,128)(2,1)S(1)}, bf16[2,127,2048]{2,0,1:T(2,128)(2,1)S(1)}, u32[]{:S(2)}, u32[]{:S(2)}) %collective-permute-start.1) | collective-permute-done | bytes 1040416 | tf_op jit(solution)/shard_map/ppermute | solution.py:17
  51.8 22.2 %collective-permute-done = bf16[2,127,2048]{2,0,1:T(2,128)(2,1)} collective-permute-done((bf16[2,127,2048]{2,0,1:T(2,128)(2,1)}, bf16[2,127,2048]{2,0,1:T(2,128)(2,1)}, u32[]{:S(2)}, u32[]{:S(2)}) %collective-permute-start) | collective-permute-done | bytes 1040416 | tf_op jit(solution)/shard_map/ppermute | solution.py:16
  74.0 1.6 copy.10
  75.8 1.1 broadcast.3
  76.9 99.7 %while.34 = (s32[]{:T(128)}, f32[128,2048]{1,0:T(8,128)}, f32[128,2048]{1,0:T(8,128)}, f32[128,2048]{1,0:T(8,128)}, bf16[255,2048]{1,0:T(8,128)(2,1)S(1)}, /*ind...) while((s32[]{:T(128)}, f32[128,2048]{1,0:T(8,128)}, ...), condition=%wide.region_17.0_spmd.clone, body=%wide.region_0.0_spmd.clone.sunk | while | flops 25657384 | bytes 22545316 | solution.py:39
  76.9 1.6 constant_dynamic-slice_fusion.34
  78.6 4.3 %fusion.58 = f32[128,2048]{1,0:T(8,128)} fusion(f32[128,2048]{1,0:T(8,128)} %get-tuple-element.655, f32[2048]{0:T(1024)S(1)} %bitcast.168, f32[2048]{0:T(1024)S(1)} %bitcast.154, f32[2048]{0:T(1024)S(1)} %bitcast.155, f32[2048]{0:T(1024)S(1)} %bitcast.156, f32[2048]{0:T(1024)S(1)} %bitcast.157, f32[2048]{0:T(1024)S(1)} %bitcast.158, ...), kind=kLoop, calls=%fused_computation.47.clone.1 | loop fusion | flops 12845056 | bytes 10616897 | tf_op jit(solution)/shard_map/while/body/eval_jaxpr/add | solution.py:33
  82.9 4.5 %fusion.59 = (f32[2048]{0:T(1024)S(1)}, f32[2048]{0:T(1024)S(1)}, f32[2048]{0:T(1024)S(1)}, f32[2048]{0:T(1024)S(1)}, f32[2048]{0:T(1024)S(1)}, /*index=5*/f32[2...) fusion(bf16[128,2048]{1,0:T(8,128)(2,1)S(1)} %copy-done.3, ...), kind=kLoop, calls=%fused_computation.63.clone.1 | loop fusion | flops 12812288 | bytes 9044032 | tf_op jit(solution)/shard_map/while/body/eval_jaxpr/reduce_sum | solution.py:34
  88.2 1.9 constant_dynamic-slice_fusion.34
  90.1 5.5 %fusion.58 = f32[128,2048]{1,0:T(8,128)} fusion(f32[128,2048]{1,0:T(8,128)} %get-tuple-element.655, f32[2048]{0:T(1024)S(1)} %bitcast.168, f32[2048]{0:T(1024)S(1)} %bitcast.154, f32[2048]{0:T(1024)S(1)} %bitcast.155, f32[2048]{0:T(1024)S(1)} %bitcast.156, f32[2048]{0:T(1024)S(1)} %bitcast.157, f32[2048]{0:T(1024)S(1)} %bitcast.158, ...), kind=kLoop, calls=%fused_computation.47.clone.1 | loop fusion | flops 12845056 | bytes 10616897 | tf_op jit(solution)/shard_map/while/body/eval_jaxpr/add | solution.py:33
  95.7 4.5 %fusion.59 = (f32[2048]{0:T(1024)S(1)}, f32[2048]{0:T(1024)S(1)}, f32[2048]{0:T(1024)S(1)}, f32[2048]{0:T(1024)S(1)}, f32[2048]{0:T(1024)S(1)}, /*index=5*/f32[2...) fusion(bf16[128,2048]{1,0:T(8,128)(2,1)S(1)} %copy-done.3, ...), kind=kLoop, calls=%fused_computation.63.clone.1 | loop fusion | flops 12812288 | bytes 9044032 | tf_op jit(solution)/shard_map/while/body/eval_jaxpr/reduce_sum | solution.py:34
  101.0 1.6 constant_dynamic-slice_fusion.34
  102.6 5.5 %fusion.58 = f32[128,2048]{1,0:T(8,128)} fusion(f32[128,2048]{1,0:T(8,128)} %get-tuple-element.655, f32[2048]{0:T(1024)S(1)} %bitcast.168, f32[2048]{0:T(1024)S(1)} %bitcast.154, f32[2048]{0:T(1024)S(1)} %bitcast.155, f32[2048]{0:T(1024)S(1)} %bitcast.156, f32[2048]{0:T(1024)S(1)} %bitcast.157, f32[2048]{0:T(1024)S(1)} %bitcast.158, ...), kind=kLoop, calls=%fused_computation.47.clone.1 | loop fusion | flops 12845056 | bytes 10616897 | tf_op jit(solution)/shard_map/while/body/eval_jaxpr/add | solution.py:33
  108.2 4.5 %fusion.59 = (f32[2048]{0:T(1024)S(1)}, f32[2048]{0:T(1024)S(1)}, f32[2048]{0:T(1024)S(1)}, f32[2048]{0:T(1024)S(1)}, f32[2048]{0:T(1024)S(1)}, /*index=5*/f32[2...) fusion(bf16[128,2048]{1,0:T(8,128)(2,1)S(1)} %copy-done.3, ...), kind=kLoop, calls=%fused_computation.63.clone.1 | loop fusion | flops 12812288 | bytes 9044032 | tf_op jit(solution)/shard_map/while/body/eval_jaxpr/reduce_sum | solution.py:34
  112.9 0.7 constant_dynamic-update-slice_fusion.2
  113.5 1.6 constant_dynamic-slice_fusion.34
  115.2 5.5 %fusion.58 = f32[128,2048]{1,0:T(8,128)} fusion(f32[128,2048]{1,0:T(8,128)} %get-tuple-element.655, f32[2048]{0:T(1024)S(1)} %bitcast.168, f32[2048]{0:T(1024)S(1)} %bitcast.154, f32[2048]{0:T(1024)S(1)} %bitcast.155, f32[2048]{0:T(1024)S(1)} %bitcast.156, f32[2048]{0:T(1024)S(1)} %bitcast.157, f32[2048]{0:T(1024)S(1)} %bitcast.158, ...), kind=kLoop, calls=%fused_computation.47.clone.1 | loop fusion | flops 12845056 | bytes 10616897 | tf_op jit(solution)/shard_map/while/body/eval_jaxpr/add | solution.py:33
  120.7 4.5 %fusion.59 = (f32[2048]{0:T(1024)S(1)}, f32[2048]{0:T(1024)S(1)}, f32[2048]{0:T(1024)S(1)}, f32[2048]{0:T(1024)S(1)}, f32[2048]{0:T(1024)S(1)}, /*index=5*/f32[2...) fusion(bf16[128,2048]{1,0:T(8,128)(2,1)S(1)} %copy-done.3, ...), kind=kLoop, calls=%fused_computation.63.clone.1 | loop fusion | flops 12812288 | bytes 9044032 | tf_op jit(solution)/shard_map/while/body/eval_jaxpr/reduce_sum | solution.py:34
  125.4 0.7 constant_dynamic-update-slice_fusion.2
  126.1 1.6 constant_dynamic-slice_fusion.34
  127.7 5.5 %fusion.58 = f32[128,2048]{1,0:T(8,128)} fusion(f32[128,2048]{1,0:T(8,128)} %get-tuple-element.655, f32[2048]{0:T(1024)S(1)} %bitcast.168, f32[2048]{0:T(1024)S(1)} %bitcast.154, f32[2048]{0:T(1024)S(1)} %bitcast.155, f32[2048]{0:T(1024)S(1)} %bitcast.156, f32[2048]{0:T(1024)S(1)} %bitcast.157, f32[2048]{0:T(1024)S(1)} %bitcast.158, ...), kind=kLoop, calls=%fused_computation.47.clone.1 | loop fusion | flops 12845056 | bytes 10616897 | tf_op jit(solution)/shard_map/while/body/eval_jaxpr/add | solution.py:33
  133.3 4.5 %fusion.59 = (f32[2048]{0:T(1024)S(1)}, f32[2048]{0:T(1024)S(1)}, f32[2048]{0:T(1024)S(1)}, f32[2048]{0:T(1024)S(1)}, f32[2048]{0:T(1024)S(1)}, /*index=5*/f32[2...) fusion(bf16[128,2048]{1,0:T(8,128)(2,1)S(1)} %copy-done.3, ...), kind=kLoop, calls=%fused_computation.63.clone.1 | loop fusion | flops 12812288 | bytes 9044032 | tf_op jit(solution)/shard_map/while/body/eval_jaxpr/reduce_sum | solution.py:34
  138.0 0.7 constant_dynamic-update-slice_fusion.2
  138.6 1.6 constant_dynamic-slice_fusion.34
  140.3 5.5 %fusion.58 = f32[128,2048]{1,0:T(8,128)} fusion(f32[128,2048]{1,0:T(8,128)} %get-tuple-element.655, f32[2048]{0:T(1024)S(1)} %bitcast.168, f32[2048]{0:T(1024)S(1)} %bitcast.154, f32[2048]{0:T(1024)S(1)} %bitcast.155, f32[2048]{0:T(1024)S(1)} %bitcast.156, f32[2048]{0:T(1024)S(1)} %bitcast.157, f32[2048]{0:T(1024)S(1)} %bitcast.158, ...), kind=kLoop, calls=%fused_computation.47.clone.1 | loop fusion | flops 12845056 | bytes 10616897 | tf_op jit(solution)/shard_map/while/body/eval_jaxpr/add | solution.py:33
  145.8 4.5 %fusion.59 = (f32[2048]{0:T(1024)S(1)}, f32[2048]{0:T(1024)S(1)}, f32[2048]{0:T(1024)S(1)}, f32[2048]{0:T(1024)S(1)}, f32[2048]{0:T(1024)S(1)}, /*index=5*/f32[2...) fusion(bf16[128,2048]{1,0:T(8,128)(2,1)S(1)} %copy-done.3, ...), kind=kLoop, calls=%fused_computation.63.clone.1 | loop fusion | flops 12812288 | bytes 9044032 | tf_op jit(solution)/shard_map/while/body/eval_jaxpr/reduce_sum | solution.py:34
  150.5 0.7 constant_dynamic-update-slice_fusion.2
  151.2 1.6 constant_dynamic-slice_fusion.34
  152.9 5.5 %fusion.58 = f32[128,2048]{1,0:T(8,128)} fusion(f32[128,2048]{1,0:T(8,128)} %get-tuple-element.655, f32[2048]{0:T(1024)S(1)} %bitcast.168, f32[2048]{0:T(1024)S(1)} %bitcast.154, f32[2048]{0:T(1024)S(1)} %bitcast.155, f32[2048]{0:T(1024)S(1)} %bitcast.156, f32[2048]{0:T(1024)S(1)} %bitcast.157, f32[2048]{0:T(1024)S(1)} %bitcast.158, ...), kind=kLoop, calls=%fused_computation.47.clone.1 | loop fusion | flops 12845056 | bytes 10616897 | tf_op jit(solution)/shard_map/while/body/eval_jaxpr/add | solution.py:33
  158.4 4.5 %fusion.59 = (f32[2048]{0:T(1024)S(1)}, f32[2048]{0:T(1024)S(1)}, f32[2048]{0:T(1024)S(1)}, f32[2048]{0:T(1024)S(1)}, f32[2048]{0:T(1024)S(1)}, /*index=5*/f32[2...) fusion(bf16[128,2048]{1,0:T(8,128)(2,1)S(1)} %copy-done.3, ...), kind=kLoop, calls=%fused_computation.63.clone.1 | loop fusion | flops 12812288 | bytes 9044032 | tf_op jit(solution)/shard_map/while/body/eval_jaxpr/reduce_sum | solution.py:34
  163.1 0.7 constant_dynamic-update-slice_fusion.2
  163.8 1.9 constant_dynamic-slice_fusion.34
  165.7 5.5 %fusion.58 = f32[128,2048]{1,0:T(8,128)} fusion(f32[128,2048]{1,0:T(8,128)} %get-tuple-element.655, f32[2048]{0:T(1024)S(1)} %bitcast.168, f32[2048]{0:T(1024)S(1)} %bitcast.154, f32[2048]{0:T(1024)S(1)} %bitcast.155, f32[2048]{0:T(1024)S(1)} %bitcast.156, f32[2048]{0:T(1024)S(1)} %bitcast.157, f32[2048]{0:T(1024)S(1)} %bitcast.158, ...), kind=kLoop, calls=%fused_computation.47.clone.1 | loop fusion | flops 12845056 | bytes 10616897 | tf_op jit(solution)/shard_map/while/body/eval_jaxpr/add | solution.py:33
  171.2 4.5 %fusion.59 = (f32[2048]{0:T(1024)S(1)}, f32[2048]{0:T(1024)S(1)}, f32[2048]{0:T(1024)S(1)}, f32[2048]{0:T(1024)S(1)}, f32[2048]{0:T(1024)S(1)}, /*index=5*/f32[2...) fusion(bf16[128,2048]{1,0:T(8,128)(2,1)S(1)} %copy-done.3, ...), kind=kLoop, calls=%fused_computation.63.clone.1 | loop fusion | flops 12812288 | bytes 9044032 | tf_op jit(solution)/shard_map/while/body/eval_jaxpr/reduce_sum | solution.py:34
  175.9 0.7 constant_dynamic-update-slice_fusion.2
  176.6 41.7 %while.35 = (s32[]{:T(128)}, f32[128,2048]{1,0:T(8,128)S(1)}, f32[128,2048]{1,0:T(8,128)}, bf16[255,2048]{1,0:T(8,128)(2,1)S(1)}, s32[]{:T(128)}, /*index=5*/s32...) while((s32[]{:T(128)}, f32[128,2048]{1,0:T(8,128)S(1)}, ...), condition=%wide.region_19.0_spmd.clone, body=%wide.region_18.0_spmd.clone.sunk | while | flops 12845095 | bytes 10879766 | solution.py:55
  176.9 1.7 constant_dynamic-slice_fusion.35
  178.6 3.4 %fusion.60 = f32[128,2048]{1,0:T(8,128)S(1)} fusion(f32[128,2048]{1,0:T(8,128)S(1)} %get-tuple-element.580, bf16[255,2048]{1,0:T(8,128)(2,1)S(1)} %get-tuple-element.606, s32[]{:T(128)S(6)} %add.1191, s32[]{:T(128)S(6)} %add.1192, s32[]{:T(128)S(6)} %add.1193, s32[]{:T(128)S(6)} %add.1194, s32[]{:T(128)S(6)} %add.1195, s32[]{:T(128)S(6)} %add.1196, ...), kind=kLoop, calls=%fused_computation.96.clone.1 | loop fusion | flops 12845056 | bytes 10616897 | tf_op jit(solution)/shard_map/while/body/eval_jaxpr/add | solution.py:50
  182.0 1.9 constant_dynamic-slice_fusion.35
  183.9 3.4 %fusion.60 = f32[128,2048]{1,0:T(8,128)S(1)} fusion(f32[128,2048]{1,0:T(8,128)S(1)} %get-tuple-element.580, bf16[255,2048]{1,0:T(8,128)(2,1)S(1)} %get-tuple-element.606, s32[]{:T(128)S(6)} %add.1191, s32[]{:T(128)S(6)} %add.1192, s32[]{:T(128)S(6)} %add.1193, s32[]{:T(128)S(6)} %add.1194, s32[]{:T(128)S(6)} %add.1195, s32[]{:T(128)S(6)} %add.1196, ...), kind=kLoop, calls=%fused_computation.96.clone.1 | loop fusion | flops 12845056 | bytes 10616897 | tf_op jit(solution)/shard_map/while/body/eval_jaxpr/add | solution.py:50
  187.4 1.7 constant_dynamic-slice_fusion.35
  189.1 3.4 %fusion.60 = f32[128,2048]{1,0:T(8,128)S(1)} fusion(f32[128,2048]{1,0:T(8,128)S(1)} %get-tuple-element.580, bf16[255,2048]{1,0:T(8,128)(2,1)S(1)} %get-tuple-element.606, s32[]{:T(128)S(6)} %add.1191, s32[]{:T(128)S(6)} %add.1192, s32[]{:T(128)S(6)} %add.1193, s32[]{:T(128)S(6)} %add.1194, s32[]{:T(128)S(6)} %add.1195, s32[]{:T(128)S(6)} %add.1196, ...), kind=kLoop, calls=%fused_computation.96.clone.1 | loop fusion | flops 12845056 | bytes 10616897 | tf_op jit(solution)/shard_map/while/body/eval_jaxpr/add | solution.py:50
  192.5 1.7 constant_dynamic-slice_fusion.35
  194.2 3.4 %fusion.60 = f32[128,2048]{1,0:T(8,128)S(1)} fusion(f32[128,2048]{1,0:T(8,128)S(1)} %get-tuple-element.580, bf16[255,2048]{1,0:T(8,128)(2,1)S(1)} %get-tuple-element.606, s32[]{:T(128)S(6)} %add.1191, s32[]{:T(128)S(6)} %add.1192, s32[]{:T(128)S(6)} %add.1193, s32[]{:T(128)S(6)} %add.1194, s32[]{:T(128)S(6)} %add.1195, s32[]{:T(128)S(6)} %add.1196, ...), kind=kLoop, calls=%fused_computation.96.clone.1 | loop fusion | flops 12845056 | bytes 10616897 | tf_op jit(solution)/shard_map/while/body/eval_jaxpr/add | solution.py:50
  197.6 1.7 constant_dynamic-slice_fusion.35
  199.3 3.4 %fusion.60 = f32[128,2048]{1,0:T(8,128)S(1)} fusion(f32[128,2048]{1,0:T(8,128)S(1)} %get-tuple-element.580, bf16[255,2048]{1,0:T(8,128)(2,1)S(1)} %get-tuple-element.606, s32[]{:T(128)S(6)} %add.1191, s32[]{:T(128)S(6)} %add.1192, s32[]{:T(128)S(6)} %add.1193, s32[]{:T(128)S(6)} %add.1194, s32[]{:T(128)S(6)} %add.1195, s32[]{:T(128)S(6)} %add.1196, ...), kind=kLoop, calls=%fused_computation.96.clone.1 | loop fusion | flops 12845056 | bytes 10616897 | tf_op jit(solution)/shard_map/while/body/eval_jaxpr/add | solution.py:50
  202.7 1.7 constant_dynamic-slice_fusion.35
  204.4 3.4 %fusion.60 = f32[128,2048]{1,0:T(8,128)S(1)} fusion(f32[128,2048]{1,0:T(8,128)S(1)} %get-tuple-element.580, bf16[255,2048]{1,0:T(8,128)(2,1)S(1)} %get-tuple-element.606, s32[]{:T(128)S(6)} %add.1191, s32[]{:T(128)S(6)} %add.1192, s32[]{:T(128)S(6)} %add.1193, s32[]{:T(128)S(6)} %add.1194, s32[]{:T(128)S(6)} %add.1195, s32[]{:T(128)S(6)} %add.1196, ...), kind=kLoop, calls=%fused_computation.96.clone.1 | loop fusion | flops 12845056 | bytes 10616897 | tf_op jit(solution)/shard_map/while/body/eval_jaxpr/add | solution.py:50
  207.8 1.7 constant_dynamic-slice_fusion.35
  209.6 3.4 %fusion.60 = f32[128,2048]{1,0:T(8,128)S(1)} fusion(f32[128,2048]{1,0:T(8,128)S(1)} %get-tuple-element.580, bf16[255,2048]{1,0:T(8,128)(2,1)S(1)} %get-tuple-element.606, s32[]{:T(128)S(6)} %add.1191, s32[]{:T(128)S(6)} %add.1192, s32[]{:T(128)S(6)} %add.1193, s32[]{:T(128)S(6)} %add.1194, s32[]{:T(128)S(6)} %add.1195, s32[]{:T(128)S(6)} %add.1196, ...), kind=kLoop, calls=%fused_computation.96.clone.1 | loop fusion | flops 12845056 | bytes 10616897 | tf_op jit(solution)/shard_map/while/body/eval_jaxpr/add | solution.py:50
  213.0 2.0 constant_dynamic-slice_fusion.35
  214.9 3.4 %fusion.60 = f32[128,2048]{1,0:T(8,128)S(1)} fusion(f32[128,2048]{1,0:T(8,128)S(1)} %get-tuple-element.580, bf16[255,2048]{1,0:T(8,128)(2,1)S(1)} %get-tuple-element.606, s32[]{:T(128)S(6)} %add.1191, s32[]{:T(128)S(6)} %add.1192, s32[]{:T(128)S(6)} %add.1193, s32[]{:T(128)S(6)} %add.1194, s32[]{:T(128)S(6)} %add.1195, s32[]{:T(128)S(6)} %add.1196, ...), kind=kLoop, calls=%fused_computation.96.clone.1 | loop fusion | flops 12845056 | bytes 10616897 | tf_op jit(solution)/shard_map/while/body/eval_jaxpr/add | solution.py:50
  218.4 2.7 %fusion.49 = (bf16[128,2048]{1,0:T(8,128)(2,1)}, bf16[128,2048]{1,0:T(8,128)(2,1)}, bf16[128,2048]{1,0:T(8,128)(2,1)}) fusion(f32[128,2048]{1,0:T(8,128)S(1)} %get-tuple-element.284, bf16[128,2048]{1,0:T(8,128)(2,1)} %param.10, bf16[128,2048]{1,0:T(8,128)(2,1)} %param.11, f32[128,2048]{1,0:T(8,128)S(1)} %copy-done, ...), kind=kLoop, calls=%fused_computation.120 | loop fusion | flops 2359296 | bytes 5242884 | tf_op jit(solution)/shard_map/convert_element_type | solution.py:75
  221.1 34.8 %all-reduce.2.cloned.1.call-done = f32[128,2048]{1,0:T(8,128)} async-done(((f32[128,2048]{1,0:T(8,128)}), f32[128,2048]{1,0:T(8,128)}) %all-reduce.2.cloned.1.call-update) | async-done | bytes 1048592 | tf_op jit(solution)/shard_map/psum | solution.py:77
  255.9 2.1 multiply_convert_fusion
  (46 shorter events, 4.6 us)
Async XLA Ops:
  7.2 14.2 %copy-start.6 = (bf16[128,2048]{1,0:T(8,128)(2,1)S(1)}, bf16[128,2048]{1,0:T(8,128)(2,1)}, u32[]{:S(2)}) copy-start(bf16[128,2048]{1,0:T(8,128)(2,1)} %param.9) | copy-start | bytes 1572868
  7.2 14.1 %all-gather.2.cloned.1.call-start = ((), (), s32[]{:S(2)}) async-start(), calls=%async_computation | async-start | bytes 1572864 | tf_op jit(solution)/shard_map/all_gather | solution.py:62
  7.9 248.0 %all-reduce.2.cloned.1.call-start = ((), (), s32[]{:S(2)}) async-start(), calls=%async_computation.1 | async-start | bytes 2097152 | tf_op jit(solution)/shard_map/psum | solution.py:77
  9.3 13.6 %copy-start.4 = (bf16[1,128,2048]{2,1,0:T(8,128)(2,1)}, bf16[1,128,2048]{2,1,0:T(8,128)(2,1)S(1)}, u32[]{:S(2)}) copy-start(bf16[1,128,2048]{2,1,0:T(8,128)(2,1)S(1)} %fusion.54) | copy-start | bytes 1572868
  22.5 0.8 copy-start.1
  24.4 27.1 %collective-permute-start.1 = (bf16[2,127,2048]{2,0,1:T(2,128)(2,1)S(1)}, bf16[2,127,2048]{2,0,1:T(2,128)(2,1)S(1)}, u32[]{:S(2)}, u32[]{:S(2)}) collective-permute-start(bf16[2,127,2048]{2,0,1:T(2,128)(2,1)S(1)} %copy.11), channel_id=1, source_target_pairs={{2,0},{4,2},{6,4},{8,6},{10,8},{12,10},{14,12},{3,1},{5,3},{7,5},{... | collective-permute-start | bytes 3121160 | tf_op jit(solution)/shard_map/ppermute | solution.py:17
  27.7 46.3 %collective-permute-start = (bf16[2,127,2048]{2,0,1:T(2,128)(2,1)}, bf16[2,127,2048]{2,0,1:T(2,128)(2,1)}, u32[]{:S(2)}, u32[]{:S(2)}) collective-permute-start(bf16[2,127,2048]{2,0,1:T(2,128)(2,1)} %copy.9), channel_id=1, source_target_pairs={{0,2},{2,4},{4,6},{6,8},{8,10},{10,12},{12,14},{1,3},{3,5},{5,7},{... | collective-permute-start | bytes 3121160 | tf_op jit(solution)/shard_map/ppermute | solution.py:16
  51.8 23.8 %copy-start.2 = (bf16[128,2048]{1,0:T(8,128)(2,1)S(1)}, bf16[128,2048]{1,0:T(8,128)(2,1)}, u32[]{:S(2)}) copy-start(bf16[128,2048]{1,0:T(8,128)(2,1)} %copy-done.1) | copy-start | bytes 1572868
  51.8 23.8 %copy-start.5 = (bf16[1,128,2048]{2,1,0:T(8,128)(2,1)S(1)}, bf16[1,128,2048]{2,1,0:T(8,128)(2,1)}, u32[]{:S(2)}) copy-start(bf16[1,128,2048]{2,1,0:T(8,128)(2,1)} %copy-done.4) | copy-start | bytes 1572868
  78.6 4.3 %copy-start.3 = (bf16[128,2048]{1,0:T(8,128)(2,1)S(1)}, bf16[128,2048]{1,0:T(8,128)(2,1)}, u32[]{:S(2)}) copy-start(bf16[128,2048]{1,0:T(8,128)(2,1)} %get-tuple-element.686) | copy-start | bytes 1572868 | tf_op jit(solution)/shard_map/while
  90.1 5.6 %copy-start.3 = (bf16[128,2048]{1,0:T(8,128)(2,1)S(1)}, bf16[128,2048]{1,0:T(8,128)(2,1)}, u32[]{:S(2)}) copy-start(bf16[128,2048]{1,0:T(8,128)(2,1)} %get-tuple-element.686) | copy-start | bytes 1572868 | tf_op jit(solution)/shard_map/while
  102.6 5.6 %copy-start.3 = (bf16[128,2048]{1,0:T(8,128)(2,1)S(1)}, bf16[128,2048]{1,0:T(8,128)(2,1)}, u32[]{:S(2)}) copy-start(bf16[128,2048]{1,0:T(8,128)(2,1)} %get-tuple-element.686) | copy-start | bytes 1572868 | tf_op jit(solution)/shard_map/while
  115.2 5.6 %copy-start.3 = (bf16[128,2048]{1,0:T(8,128)(2,1)S(1)}, bf16[128,2048]{1,0:T(8,128)(2,1)}, u32[]{:S(2)}) copy-start(bf16[128,2048]{1,0:T(8,128)(2,1)} %get-tuple-element.686) | copy-start | bytes 1572868 | tf_op jit(solution)/shard_map/while
  127.7 5.6 %copy-start.3 = (bf16[128,2048]{1,0:T(8,128)(2,1)S(1)}, bf16[128,2048]{1,0:T(8,128)(2,1)}, u32[]{:S(2)}) copy-start(bf16[128,2048]{1,0:T(8,128)(2,1)} %get-tuple-element.686) | copy-start | bytes 1572868 | tf_op jit(solution)/shard_map/while
  140.3 5.6 %copy-start.3 = (bf16[128,2048]{1,0:T(8,128)(2,1)S(1)}, bf16[128,2048]{1,0:T(8,128)(2,1)}, u32[]{:S(2)}) copy-start(bf16[128,2048]{1,0:T(8,128)(2,1)} %get-tuple-element.686) | copy-start | bytes 1572868 | tf_op jit(solution)/shard_map/while
  152.9 5.6 %copy-start.3 = (bf16[128,2048]{1,0:T(8,128)(2,1)S(1)}, bf16[128,2048]{1,0:T(8,128)(2,1)}, u32[]{:S(2)}) copy-start(bf16[128,2048]{1,0:T(8,128)(2,1)} %get-tuple-element.686) | copy-start | bytes 1572868 | tf_op jit(solution)/shard_map/while
  165.7 5.6 %copy-start.3 = (bf16[128,2048]{1,0:T(8,128)(2,1)S(1)}, bf16[128,2048]{1,0:T(8,128)(2,1)}, u32[]{:S(2)}) copy-start(bf16[128,2048]{1,0:T(8,128)(2,1)} %get-tuple-element.686) | copy-start | bytes 1572868 | tf_op jit(solution)/shard_map/while
  176.6 41.7 %copy-start = (f32[128,2048]{1,0:T(8,128)S(1)}, f32[128,2048]{1,0:T(8,128)}, u32[]{:S(2)}) copy-start(f32[128,2048]{1,0:T(8,128)} %get-tuple-element.283) | copy-start | bytes 3145732
Sparse Core Ops, SparseCore 0:
  9.6 11.7 all-gather.1
  176.7 79.0 all-reduce.1
where the time goes:
time: 267 us; the launch traced here: 265 us
  other arithmetic  116 us (43%)
  waiting for transfers between devices  85.7 us (32%)
  local copies, waits for them, and re-layouts  41.1 us (15%)
  between operations  14.2 us (5%)
  starting transfers between devices  6.89 us (3%)
    add x8, other arithmetic, forward_stepper(): mixture = mixture + coeffs[within] * shifted  43.1 us
    reduce_sum x8, other arithmetic, forward_stepper(): sums_list.append(jnp.sum(gated.astype(jnp.float32) * shifted, axis=0))  35.7 us
    psum x1, waiting for transfers between devices, local(): totals = lax.psum(tap_rows, 'ctx')  34.8 us
    add x8, other arithmetic, backward_stepper(): spread + coeffs[within] * window[within:within + tok_rows].astype(jnp.flo...  27.2 us
    ppermute x1, waiting for transfers between devices, extended_2(): before = lax.ppermute(last, axis, up)  22.2 us
    ppermute x1, waiting for transfers between devices, extended_2(): after = lax.ppermute(leading, axis, down)  16 us
    slice x8, local copies, waits for them, and re-layouts, backward_stepper(): coeffs[within] * window[within:within + tok_rows].astype(jnp.float32)  14 us
    slice x8, local copies, waits for them, and re-layouts, forward_stepper(): mixture = mixture + coeffs[within] * shifted  13.5 us
  transfers between devices with their start and end apart: 4, of which 4 were waited for; matrix products, arithmetic and copies ran while one was open for 19% of the time, Pallas kernels for 0%

commit v1 on v0

v1 whole, which is shorter than its diff:
```python
import functools
import math

import jax
import jax.numpy as jnp
import ml_dtypes
import numpy as np
from jax import lax
from jax.experimental import pallas as pl
from jax.experimental.pallas import tpu as pltpu
from jax.sharding import PartitionSpec as P

MESH = pl.DeviceIdType.MESH
F32 = jnp.float32
BF16 = jnp.bfloat16
WIDTH = 512
DIRECT_PEERS = 8


def split(matrix):
    high = matrix.astype(ml_dtypes.bfloat16)
    low = (matrix - high.astype(np.float64)).astype(ml_dtypes.bfloat16)
    return np.concatenate([high, low], axis=0)


def transforms(length):
    half = length // 2
    turns = (2 * np.arange(half)[:, None] + 1) * np.arange(length)[None, :] % (2 * length)
    angle = np.pi * turns / length
    forward = np.concatenate([np.cos(angle), -np.sin(angle)], axis=0)
    inverse = forward.T / half
    return split(forward), split(inverse[:half]), split(inverse[half:])


def spectrum(matrix, rows):
    both = jnp.dot(matrix, rows, preferred_element_type=F32)
    half = both.shape[0] // 2
    return both[:half] + both[half:]


def restore(matrix, freqs):
    half = matrix.shape[0] // 2
    high = freqs.astype(BF16)
    low = (freqs - high.astype(F32)).astype(BF16)
    both = jnp.dot(matrix, high, preferred_element_type=F32)
    extra = jnp.dot(matrix[:half], low, preferred_element_type=F32)
    return both[:half] + both[half:] + extra


def times(a, b):
    half = a.shape[0] // 2
    ar, ai, br, bi = a[:half], a[half:], b[:half], b[half:]
    return jnp.concatenate([ar * br - ai * bi, ar * bi + ai * br], axis=0)


def times_conj(a, b):
    half = a.shape[0] // 2
    ar, ai, br, bi = a[:half], a[half:], b[:half], b[half:]
    return jnp.concatenate([ar * br + ai * bi, ai * br - ar * bi], axis=0)


def kernel(
    peers, direct, scale,
    q_ref, k_ref, v_ref, og_ref, h_ref, fwd_ref, inv0_ref, inv1_ref,
    dq_ref, dk_ref, dv_ref, df_ref,
    up, prod, gate, before, after, part, parts_in, hspec,
    up_sems, halo_send, halo_recv, rs_send, rs_recv, ag_send, ag_recv,
):
    grp, me, core = (lax.axis_index(a) for a in ("grp", "ctx", "tp"))
    rows, channels = q_ref.shape
    taps = h_ref.shape[0]
    chunks = channels // WIDTH
    mine = rows // 2
    has_before, has_after = me > 0, me < peers - 1

    def at(other):
        return (grp, other, core)

    barrier = pltpu.get_barrier_semaphore()
    pl.semaphore_signal(barrier, inc=1, device_id=(grp, me, 1 - core), device_id_type=MESH)
    if direct:
        for step in range(1, peers):
            pl.semaphore_signal(
                barrier, inc=1, device_id=at(lax.rem(me + step, peers)), device_id_type=MESH
            )
        pl.semaphore_wait(barrier, peers)
    else:
        for step in (1, peers - 1):
            pl.semaphore_signal(
                barrier, inc=1, device_id=at(lax.rem(me + step, peers)), device_id_type=MESH
            )
        pl.semaphore_wait(barrier, 3)

    def columns(index):
        return pl.ds(pl.multiple_of(index * WIDTH, WIDTH), WIDTH)

    def up_copies():
        own = up.at[pl.ds(pl.multiple_of(core * mine, mine), mine)]
        near = og_ref.at[:, pl.ds(pl.multiple_of(core * channels, channels), channels)]
        far = og_ref.at[:, pl.ds(pl.multiple_of((1 - core) * channels, channels), channels)]
        local = pltpu.make_async_copy(near, own, up_sems.at[0])
        remote = pltpu.make_async_remote_copy(
            src_ref=far, dst_ref=own, send_sem=up_sems.at[1], recv_sem=up_sems.at[2],
            device_id=(grp, me, 1 - core), device_id_type=MESH,
        )
        return local, remote

    def upward(index):
        return pltpu.make_async_remote_copy(
            src_ref=prod.at[index], dst_ref=before.at[index],
            send_sem=halo_send.at[0, index], recv_sem=halo_recv.at[0, index],
            device_id=at(lax.rem(me + 1, peers)), device_id_type=MESH,
        )

    def downward(index):
        return pltpu.make_async_remote_copy(
            src_ref=gate.at[index], dst_ref=after.at[index],
            send_sem=halo_send.at[1, index], recv_sem=halo_recv.at[1, index],
            device_id=at(lax.rem(me + peers - 1, peers)), device_id_type=MESH,
        )

    for copy in up_copies():
        copy.start()

    @pl.loop(0, chunks)
    def _(index):
        cols = columns(index)
        prod[index] = (k_ref[:, cols].astype(F32) * v_ref[:, cols].astype(F32)).astype(BF16)

        @pl.when(has_after)
        def _():
            upward(index).start()

    for copy in up_copies():
        copy.wait()

    @pl.loop(0, chunks)
    def _(index):
        cols = columns(index)
        gate[index] = (up[:, cols].astype(F32) * q_ref[:, cols].astype(F32)).astype(BF16)

        @pl.when(has_before)
        def _():
            downward(index).start()

        @pl.when(jnp.logical_not(has_before))
        def _():
            before[index] = jnp.zeros((rows, WIDTH), BF16)

        @pl.when(jnp.logical_not(has_after))
        def _():
            after[index] = jnp.zeros((rows, WIDTH), BF16)

        hspec[index] = spectrum(fwd_ref[:, :taps], h_ref[:, cols])

    share = taps // peers if direct else taps

    def scatter(step, index):
        owner = lax.rem(me + step, peers)
        return pltpu.make_async_remote_copy(
            src_ref=part.at[index, pl.ds(pl.multiple_of(owner * share, share), share)],
            dst_ref=parts_in.at[step - 1, index],
            send_sem=rs_send.at[step - 1, index], recv_sem=rs_recv.at[step - 1, index],
            device_id=at(owner), device_id_type=MESH,
        )

    def collect(step, index):
        block = df_ref.at[pl.ds(pl.multiple_of(me * share, share), share), columns(index)]
        return pltpu.make_async_remote_copy(
            src_ref=block, dst_ref=block,
            send_sem=ag_send.at[step - 1, index], recv_sem=ag_recv.at[step - 1, index],
            device_id=at(lax.rem(me + step, peers)), device_id_type=MESH,
        )

    @pl.loop(0, chunks)
    def _(index):
        cols = columns(index)

        @pl.when(has_before)
        def _():
            upward(index).wait_recv()

        pspec = spectrum(fwd_ref[...], jnp.concatenate([before[index], prod[index]], axis=0))
        gspec = spectrum(fwd_ref[:, rows:], gate[index])
        terms = restore(inv0_ref[...], times_conj(gspec, pspec))
        if direct:
            part[index] = terms.astype(BF16)
            for step in range(1, peers):
                scatter(step, index).start()
        else:
            df_ref[:, cols] = terms
        mixture = restore(inv1_ref[...], times(pspec, hspec[index]))
        dq_ref[:, cols] = (up[:, cols].astype(F32) * mixture).astype(BF16)

    @pl.loop(0, chunks)
    def _(index):
        cols = columns(index)

        @pl.when(has_after)
        def _():
            downward(index).wait_recv()

        gspec = spectrum(fwd_ref[...], jnp.concatenate([gate[index], after[index]], axis=0))
        spread = restore(inv0_ref[...], times_conj(gspec, hspec[index]))
        dk_ref[:, cols] = (spread * v_ref[:, cols].astype(F32)).astype(BF16)
        dv_ref[:, cols] = (spread * k_ref[:, cols].astype(F32)).astype(BF16)

    if direct:

        @pl.loop(0, chunks)
        def _(index):
            own = pl.ds(pl.multiple_of(me * share, share), share)
            total = part[index, own].astype(F32)
            for step in range(1, peers):
                scatter(step, index).wait_recv()
                total = total + parts_in[step - 1, index].astype(F32)
            df_ref[own, columns(index)] = (total * scale).astype(BF16)
            for step in range(1, peers):
                collect(step, index).start()

    @pl.loop(0, chunks)
    def _(index):
        @pl.when(has_after)
        def _():
            upward(index).wait_send()

        @pl.when(has_before)
        def _():
            downward(index).wait_send()

        if direct:
            for step in range(1, peers):
                scatter(step, index).wait_send()
            for step in range(1, peers):
                collect(step, index).wait()


def local(queries, key_proj, value_proj, out_grad, filter_taps):
    rows, channels = queries.shape
    taps = filter_taps.shape[0]
    peers = lax.axis_size("ctx")
    direct = peers <= DIRECT_PEERS
    scale = 1.0 / math.sqrt(peers * rows)
    chunks = channels // WIDTH
    matrices = [jnp.asarray(m) for m in transforms(2 * rows)]
    steps = peers - 1 if direct else 1
    share = taps // peers if direct else 16
    like = jax.ShapeDtypeStruct((rows, channels), BF16)
    vmem = pl.BlockSpec(memory_space=pltpu.VMEM)
    tile = (chunks, rows, WIDTH)
    dma = pltpu.SemaphoreType.DMA
    query_grad, key_grad, value_grad, filter_grad = pl.pallas_call(
        functools.partial(kernel, peers, direct, scale),
        name="hyena_backward",
        out_shape=[like, like, like,
                   jax.ShapeDtypeStruct((taps, channels), BF16 if direct else F32)],
        in_specs=[vmem, vmem, vmem, pl.BlockSpec(memory_space=pl.ANY)] + [vmem] * 4,
        out_specs=[vmem] * 4,
        scratch_shapes=[
            pltpu.VMEM((rows, channels), BF16),
            pltpu.VMEM(tile, BF16),
            pltpu.VMEM(tile, BF16),
            pltpu.VMEM(tile, BF16),
            pltpu.VMEM(tile, BF16),
            pltpu.VMEM((chunks, taps, WIDTH), BF16),
            pltpu.VMEM((steps, chunks, share, WIDTH), BF16),
            pltpu.VMEM((chunks, 2 * rows, WIDTH), F32),
            dma((3,)), dma((2, chunks)), dma((2, chunks)),
            dma((steps, chunks)), dma((steps, chunks)), dma((steps, chunks)), dma((steps, chunks)),
        ],
        compiler_params=pltpu.CompilerParams(
            collective_id=0, has_side_effects=True, vmem_limit_bytes=40 * 1024 * 1024
        ),
        cost_estimate=pl.CostEstimate(
            flops=20 * rows * rows * channels, bytes_accessed=18 * rows * channels,
            transcendentals=0,
        ),
    )(queries, key_proj, value_proj, out_grad, filter_taps, *matrices)
    if not direct:
        filter_grad = (lax.psum(filter_grad, "ctx") * scale).astype(BF16)
    return query_grad, key_grad, value_grad, filter_grad


def solution(mesh):
    tokens = P(("grp", "ctx"), "tp")
    return jax.shard_map(
        local,
        mesh=mesh,
        in_specs=(tokens, tokens, tokens, P(("grp", "ctx", "tp"), None), P(None, "tp")),
        out_specs=(tokens, tokens, tokens, P(None, ("grp", "tp"))),
        check_vma=False,
    )
```

time: 267 us -> 62 us (0.23)
  the two profiles are of different devices: /device:TPU:0 before, /device:TPU:24 now
where the time goes in v1:
time: 62 us; the launch traced here: 61.6 us
  Pallas kernels  49.8 us (80%)
  local copies, waits for them, and re-layouts  11.1 us (18%)
  between operations  0.66 us (1%)
    pallas_call x1, Pallas kernels, local(): pl.pallas_call(functools.partial(kernel, peers, direct, scale), name='hye...  49.8 us
    unnamed x20, local copies, waits for them, and re-layouts  11.1 us

profile of v1, /device:TPU:24, one launch (start us, length us, event | category | flops | bytes accessed | tf_op | source)
XLA Modules:
  0.0 61.6 jit_solution(13914890180783151167)
XLA Ops:
  0.6 0.0 copy-start
  0.6 1.0 %copy-done = bf16[128,2048]{1,0:T(8,128)(2,1)S(1)} copy-done((bf16[128,2048]{1,0:T(8,128)(2,1)S(1)}, bf16[128,2048]{1,0:T(8,128)(2,1)}, u32[]{:S(2)}) %copy-start) | copy-done | bytes 524312
  1.7 0.0 copy-start.1
  1.7 1.0 %copy-done.1 = bf16[128,2048]{1,0:T(8,128)(2,1)S(1)} copy-done((bf16[128,2048]{1,0:T(8,128)(2,1)S(1)}, bf16[128,2048]{1,0:T(8,128)(2,1)}, u32[]{:S(2)}) %copy-start.1) | copy-done | bytes 524312
  2.7 0.0 copy-start.2
  2.7 1.0 %copy-done.2 = bf16[128,2048]{1,0:T(8,128)(2,1)S(1)} copy-done((bf16[128,2048]{1,0:T(8,128)(2,1)S(1)}, bf16[128,2048]{1,0:T(8,128)(2,1)}, u32[]{:S(2)}) %copy-start.2) | copy-done | bytes 524312
  3.8 0.0 copy-start.3
  3.8 1.0 %copy-done.3 = bf16[64,4096]{1,0:T(8,128)(2,1)S(1)} copy-done((bf16[64,4096]{1,0:T(8,128)(2,1)S(1)}, bf16[64,4096]{1,0:T(8,128)(2,1)}, u32[]{:S(2)}) %copy-start.3) | copy-done | bytes 524312
  4.8 0.0 copy-start.4
  4.8 1.0 %copy-done.4 = bf16[128,2048]{1,0:T(8,128)(2,1)S(1)} copy-done((bf16[128,2048]{1,0:T(8,128)(2,1)S(1)}, bf16[128,2048]{1,0:T(8,128)(2,1)}, u32[]{:S(2)}) %copy-start.4) | copy-done | bytes 524312
  5.8 0.0 copy-start.5
  5.8 0.9 %copy-done.5 = bf16[512,256]{1,0:T(8,128)(2,1)S(1)} copy-done((bf16[512,256]{1,0:T(8,128)(2,1)S(1)}, bf16[512,256]{1,0:T(8,128)(2,1)}, u32[]{:S(2)}) %copy-start.5) | copy-done | bytes 262168
  6.8 0.0 copy-start.6
  6.8 0.9 %copy-done.6 = bf16[256,256]{1,0:T(8,128)(2,1)S(1)} copy-done((bf16[256,256]{1,0:T(8,128)(2,1)S(1)}, bf16[256,256]{1,0:T(8,128)(2,1)}, u32[]{:S(2)}) %copy-start.6) | copy-done | bytes 131096
  7.7 0.0 copy-start.7
  7.7 0.9 %copy-done.7 = bf16[256,256]{1,0:T(8,128)(2,1)S(1)} copy-done((bf16[256,256]{1,0:T(8,128)(2,1)S(1)}, bf16[256,256]{1,0:T(8,128)(2,1)}, u32[]{:S(2)}) %copy-start.7) | copy-done | bytes 131096
  8.6 49.8 %hyena_backward.1 = (bf16[128,2048]{1,0:T(8,128)(2,1)S(1)}, bf16[128,2048]{1,0:T(8,128)(2,1)S(1)}, bf16[128,2048]{1,0:T(8,128)(2,1)S(1)}, bf16[128,2048]{1,0:T(8,128)(2,1)S(1)}) custom-call(bf16[128,2048]{1,0:T(8,128)(2,1)S(1)} %copy-done, bf16[128,2048]{1,0:T(8,128)(2,1)S(1)} %copy-done.1, bf16[128,2048]{1,0:T(8,128)(2,1)S(1)} %copy-done.2, ...), custom_call_target="tpu_custom_call" | custom-call | flops 671088640 | bytes 4718592 | tf_op jit(solution)/shard_map/hyena_backward/pallas_call | solution.py:252
  58.4 0.8 %copy.16 = bf16[128,2048]{1,0:T(8,128)(2,1)} copy(bf16[128,2048]{1,0:T(8,128)(2,1)S(1)} %get-tuple-element.8) | data formatting | bytes 1048576
  59.2 0.8 %copy.17 = bf16[128,2048]{1,0:T(8,128)(2,1)} copy(bf16[128,2048]{1,0:T(8,128)(2,1)S(1)} %get-tuple-element.9) | data formatting | bytes 1048576
  60.0 0.8 %copy.18 = bf16[128,2048]{1,0:T(8,128)(2,1)} copy(bf16[128,2048]{1,0:T(8,128)(2,1)S(1)} %get-tuple-element.10) | data formatting | bytes 1048576
  60.8 0.8 %copy.19 = bf16[128,2048]{1,0:T(8,128)(2,1)} copy(bf16[128,2048]{1,0:T(8,128)(2,1)S(1)} %get-tuple-element.11) | data formatting | bytes 1048576
Async XLA Ops:
  0.6 1.0 %copy-start = (bf16[128,2048]{1,0:T(8,128)(2,1)S(1)}, bf16[128,2048]{1,0:T(8,128)(2,1)}, u32[]{:S(2)}) copy-start(bf16[128,2048]{1,0:T(8,128)(2,1)} %q_ref.1) | copy-start | bytes 1572868
  1.7 1.0 %copy-start.1 = (bf16[128,2048]{1,0:T(8,128)(2,1)S(1)}, bf16[128,2048]{1,0:T(8,128)(2,1)}, u32[]{:S(2)}) copy-start(bf16[128,2048]{1,0:T(8,128)(2,1)} %k_ref.1) | copy-start | bytes 1572868
  2.7 1.0 %copy-start.2 = (bf16[128,2048]{1,0:T(8,128)(2,1)S(1)}, bf16[128,2048]{1,0:T(8,128)(2,1)}, u32[]{:S(2)}) copy-start(bf16[128,2048]{1,0:T(8,128)(2,1)} %v_ref.1) | copy-start | bytes 1572868
  3.8 1.0 %copy-start.3 = (bf16[64,4096]{1,0:T(8,128)(2,1)S(1)}, bf16[64,4096]{1,0:T(8,128)(2,1)}, u32[]{:S(2)}) copy-start(bf16[64,4096]{1,0:T(8,128)(2,1)} %og_ref.1) | copy-start | bytes 1572868
  4.8 1.0 %copy-start.4 = (bf16[128,2048]{1,0:T(8,128)(2,1)S(1)}, bf16[128,2048]{1,0:T(8,128)(2,1)}, u32[]{:S(2)}) copy-start(bf16[128,2048]{1,0:T(8,128)(2,1)} %h_ref.1) | copy-start | bytes 1572868
  5.8 0.9 %copy-start.5 = (bf16[512,256]{1,0:T(8,128)(2,1)S(1)}, bf16[512,256]{1,0:T(8,128)(2,1)}, u32[]{:S(2)}) copy-start(bf16[512,256]{1,0:T(8,128)(2,1)} %constant.6.clone.fwd_ref) | copy-start | bytes 786436
  6.8 0.9 %copy-start.6 = (bf16[256,256]{1,0:T(8,128)(2,1)S(1)}, bf16[256,256]{1,0:T(8,128)(2,1)}, u32[]{:S(2)}) copy-start(bf16[256,256]{1,0:T(8,128)(2,1)} %constant.8.clone.inv1_ref) | copy-start | bytes 393220
  7.7 0.9 %copy-start.7 = (bf16[256,256]{1,0:T(8,128)(2,1)S(1)}, bf16[256,256]{1,0:T(8,128)(2,1)}, u32[]{:S(2)}) copy-start(bf16[256,256]{1,0:T(8,128)(2,1)} %constant.7.clone.inv0_ref) | copy-start | bytes 393220

commit v2 on v1

v2 whole, which is shorter than its diff:
```python
import functools
import math

import jax
import jax.numpy as jnp
import ml_dtypes
import numpy as np
from jax import lax
from jax.experimental import pallas as pl
from jax.experimental.pallas import tpu as pltpu
from jax.sharding import PartitionSpec as P

MESH = pl.DeviceIdType.MESH
F32 = jnp.float32
BF16 = jnp.bfloat16
WIDTH = 512
CUTS = 4
VMEM_LIMIT = 60 * 1024 * 1024
DIRECT_PEERS = 8
PLAN = (
    "g0 g1 g2 g3 h0 h1 h2 h3 C0 C1 s0 C2 s1 L0 C3 s2 s3 L1 P0 L2 P1 L3 P2 F0 P3 F1 D0 F2 D1 F3 D2 D3"
)


def split(matrix):
    high = matrix.astype(ml_dtypes.bfloat16)
    low = (matrix - high.astype(np.float64)).astype(ml_dtypes.bfloat16)
    return np.concatenate([high, low], axis=0)


def transforms(length):
    half = length // 2
    turns = (2 * np.arange(half)[:, None] + 1) * np.arange(length)[None, :] % (2 * length)
    angle = np.pi * turns / length
    forward = np.concatenate([np.cos(angle), -np.sin(angle)], axis=0)
    inverse = forward.T / half
    return split(forward), split(inverse[:half]), split(inverse[half:])


def spectrum(matrix, rows):
    both = jnp.dot(matrix, rows, preferred_element_type=F32)
    half = both.shape[0] // 2
    return both[:half] + both[half:]


def restore(matrix, freqs):
    half = matrix.shape[0] // 2
    high = freqs.astype(BF16)
    low = (freqs - high.astype(F32)).astype(BF16)
    both = jnp.dot(matrix, high, preferred_element_type=F32)
    extra = jnp.dot(matrix[:half], low, preferred_element_type=F32)
    return both[:half] + both[half:] + extra


def times(a, b):
    half = a.shape[0] // 2
    ar, ai, br, bi = a[:half], a[half:], b[:half], b[half:]
    return jnp.concatenate([ar * br - ai * bi, ar * bi + ai * br], axis=0)


def times_conj(a, b):
    half = a.shape[0] // 2
    ar, ai, br, bi = a[:half], a[half:], b[:half], b[half:]
    return jnp.concatenate([ar * br + ai * bi, ai * br - ar * bi], axis=0)


def kernel(
    peers, direct, scale,
    q_hbm, k_hbm, v_hbm, og_hbm, h_hbm, fwd_hbm, inv0_hbm, inv1_hbm,
    dq_hbm, dk_hbm, dv_hbm, df_hbm,
    dq_ref, dk_ref, dv_ref, df_ref, q_ref, k_ref, v_ref, h_ref, fwd_ref, inv0_ref, inv1_ref,
    up, prod, gate, before, after, part, lane_in, pair_in, pair_out, hspec,
    kv_sems, in_sems, up_sems, halo_send, halo_recv,
    lane_send, lane_recv, pair_send, pair_recv, ag_send, ag_recv, fw_send, fw_recv, out_sems,
):
    grp, me, core = (lax.axis_index(a) for a in ("grp", "ctx", "tp"))
    rows, channels = q_ref.shape
    taps = h_ref.shape[0]
    chunks = channels // WIDTH
    mine = rows // 2
    has_before, has_after = me > 0, me < peers - 1
    lanes = max(peers // 2, 1)
    place, side = me // 2, lax.rem(me, 2)
    twin = 2 * place + 1 - side

    def at(other):
        return (grp, other, core)

    def lane(step):
        return 2 * lax.rem(place + step, lanes) + side

    after_me, before_me = lax.rem(me + 1, peers), lax.rem(me + peers - 1, peers)
    barrier = pltpu.get_barrier_semaphore()
    greeted = [(grp, me, 1 - core), at(after_me), at(before_me)]
    if direct:
        greeted += [at(lane(step)) for step in range(1, lanes)]
    for device in greeted:
        pl.semaphore_signal(barrier, inc=1, device_id=device, device_id_type=MESH)

    def columns(index):
        return pl.ds(index * WIDTH, WIDTH)

    kv_loads = []
    for index in range(chunks):
        cols = columns(index)
        kv_loads.append([
            pltpu.make_async_copy(hbm.at[:, cols], ref.at[:, cols], kv_sems.at[number, index])
            for number, (hbm, ref) in enumerate([(k_hbm, k_ref), (v_hbm, v_ref)])
        ])
        for copy in kv_loads[-1]:
            copy.start()
    own_rows = up.at[pl.ds(pl.multiple_of(core * mine, mine), mine)]
    near = og_hbm.at[:, pl.ds(pl.multiple_of(core * channels, channels), channels)]
    far = og_hbm.at[:, pl.ds(pl.multiple_of((1 - core) * channels, channels), channels)]
    others = [(q_hbm, q_ref), (h_hbm, h_ref), (fwd_hbm, fwd_ref), (inv0_hbm, inv0_ref),
              (inv1_hbm, inv1_ref), (near, own_rows)]
    loads = [pltpu.make_async_copy(hbm, ref, in_sems.at[number])
             for number, (hbm, ref) in enumerate(others)]
    for copy in loads:
        copy.start()

    up_copy = pltpu.make_async_remote_copy(
        src_ref=far, dst_ref=own_rows, send_sem=up_sems.at[0], recv_sem=up_sems.at[1],
        device_id=(grp, me, 1 - core), device_id_type=MESH,
    )

    def upward(index):
        return pltpu.make_async_remote_copy(
            src_ref=prod.at[index], dst_ref=before.at[index],
            send_sem=halo_send.at[0, index], recv_sem=halo_recv.at[0, index],
            device_id=at(after_me), device_id_type=MESH,
        )

    def downward(index):
        return pltpu.make_async_remote_copy(
            src_ref=gate.at[index], dst_ref=after.at[index],
            send_sem=halo_send.at[1, index], recv_sem=halo_recv.at[1, index],
            device_id=at(before_me), device_id_type=MESH,
        )

    share = taps // lanes if direct else taps
    piece = share // 2

    def scatter(step, index):
        owner = lax.rem(place + step, lanes)
        return pltpu.make_async_remote_copy(
            src_ref=part.at[index, pl.ds(pl.multiple_of(owner * share, share), share)],
            dst_ref=lane_in.at[step - 1, index],
            send_sem=lane_send.at[step - 1, index], recv_sem=lane_recv.at[step - 1, index],
            device_id=at(lane(step)), device_id_type=MESH,
        )

    def swap(index):
        return pltpu.make_async_remote_copy(
            src_ref=pair_out.at[index], dst_ref=pair_in.at[index],
            send_sem=pair_send.at[index], recv_sem=pair_recv.at[index],
            device_id=at(twin), device_id_type=MESH,
        )

    def block(step, index):
        holder = lax.rem(place + lanes - step, lanes)
        start = pl.multiple_of(holder * share + side * piece, piece)
        return df_ref.at[pl.ds(start, piece), columns(index)]

    def collect(step, index):
        return pltpu.make_async_remote_copy(
            src_ref=block(0, index), dst_ref=block(0, index),
            send_sem=ag_send.at[step - 1, index], recv_sem=ag_recv.at[step - 1, index],
            device_id=at(lane(step)), device_id_type=MESH,
        )

    def forward(step, index):
        return pltpu.make_async_remote_copy(
            src_ref=block(step, index), dst_ref=block(step, index),
            send_sem=fw_send.at[step, index], recv_sem=fw_recv.at[step, index],
            device_id=at(twin), device_id_type=MESH,
        )

    def store(number, index):
        ref = (dq_ref, dk_ref, dv_ref, df_ref)[number]
        hbm = (dq_hbm, dk_hbm, dv_hbm, df_hbm)[number]
        cols = columns(index)
        return pltpu.make_async_copy(ref.at[:, cols], hbm.at[:, cols], out_sems.at[number, index])

    def make_product(index):
        cols = columns(index)
        for copy in kv_loads[index]:
            copy.wait()
        prod[index] = (k_ref[:, cols].astype(F32) * v_ref[:, cols].astype(F32)).astype(BF16)

    make_product(0)
    pl.semaphore_wait(barrier, len(greeted))
    up_copy.start()
    for index in range(chunks):
        if index:
            make_product(index)

        @pl.when(has_after)
        def _():
            upward(index).start()

    for copy in loads:
        copy.wait()
    up_copy.wait()

    @pl.when(jnp.logical_not(has_before))
    def _():
        before[...] = jnp.zeros_like(before)

    @pl.when(jnp.logical_not(has_after))
    def _():
        after[...] = jnp.zeros_like(after)

    def make_gate(index):
        cols = columns(index)
        gate[index] = (up[:, cols].astype(F32) * q_ref[:, cols].astype(F32)).astype(BF16)

    def send_gate(index):
        @pl.when(has_before)
        def _():
            downward(index).start()

    def first(index):
        cols = columns(index)

        @pl.when(has_before)
        def _():
            upward(index).wait_recv()

        pspec = spectrum(fwd_ref[...], jnp.concatenate([before[index], prod[index]], axis=0))
        gspec = spectrum(fwd_ref[:, rows:], gate[index])
        terms = restore(inv0_ref[...], times_conj(gspec, pspec))
        if direct:
            part[index] = terms.astype(BF16)
            for step in range(1, lanes):
                scatter(step, index).start()
        else:
            df_ref[:, cols] = terms
            store(3, index).start()
        mixture = restore(inv1_ref[...], times(pspec, hspec[index]))
        dq_ref[:, cols] = (up[:, cols].astype(F32) * mixture).astype(BF16)
        store(0, index).start()

    def second(index):
        cols = columns(index)

        @pl.when(has_after)
        def _():
            downward(index).wait_recv()

        gspec = spectrum(fwd_ref[...], jnp.concatenate([gate[index], after[index]], axis=0))
        spread = restore(inv0_ref[...], times_conj(gspec, hspec[index]))
        dk_ref[:, cols] = (spread * v_ref[:, cols].astype(F32)).astype(BF16)
        dv_ref[:, cols] = (spread * k_ref[:, cols].astype(F32)).astype(BF16)
        store(1, index).start()
        store(2, index).start()

    def lane_total(index, which):
        start = pl.multiple_of(place * share + which * piece, piece)
        total = part[index, pl.ds(start, piece)].astype(F32)
        within = pl.ds(pl.multiple_of(which * piece, piece), piece)
        for step in range(1, lanes):
            total = total + lane_in[step - 1, index, within].astype(F32)
        return total

    def reduce_lane(index):
        for step in range(1, lanes):
            scatter(step, index).wait_recv()
        pair_out[index] = lane_total(index, 1 - side).astype(BF16)
        swap(index).start()

    def reduce_pair(index):
        swap(index).wait_recv()
        total = lane_total(index, side) + pair_in[index].astype(F32)
        block(0, index)[...] = (total * scale).astype(BF16)
        for step in range(1, lanes):
            collect(step, index).start()
        forward(0, index).start()

    def pass_on(index):
        for step in range(1, lanes):
            collect(step, index).wait_recv()
            forward(step, index).start()

    def taps_spectrum(index):
        hspec[index] = spectrum(fwd_ref[:, :taps], h_ref[:, columns(index)])

    run = dict(g=make_gate, s=send_gate, h=taps_spectrum, C=first, D=second)
    if direct:
        run.update(L=reduce_lane, P=reduce_pair, F=pass_on)
    for entry in PLAN.split():
        if entry[0] in run:
            run[entry[0]](int(entry[1]))

    for index in range(chunks):
        @pl.when(has_after)
        def _():
            upward(index).wait_send()

        @pl.when(has_before)
        def _():
            downward(index).wait_send()

        if direct:
            for step in range(1, lanes):
                scatter(step, index).wait_send()
                collect(step, index).wait_send()
            swap(index).wait_send()
            for step in range(lanes):
                forward(step, index).wait()
            store(3, index).start()
    for index in range(chunks):
        for number in range(4):
            store(number, index).wait()


def deliver(*refs):
    count = len(refs) // 3
    sources, targets, held, sems = refs[:count], refs[count:2 * count], refs[2 * count:-1], refs[-1]
    loads, stores = [], []
    for i in range(count):
        rows = sources[i].shape[0] // CUTS
        for j in range(CUTS):
            part = pl.ds(j * rows, rows)
            here = held[i].at[part]
            loads.append(pltpu.make_async_copy(sources[i].at[part], here, sems.at[0, i, j]))
            stores.append(pltpu.make_async_copy(here, targets[i].at[part], sems.at[1, i, j]))
    for load in loads:
        load.start()
    for load, store in zip(loads, stores):
        load.wait()
        store.start()
    for store in stores:
        store.wait()


def local(queries, key_proj, value_proj, out_grad, filter_taps):
    rows, channels = queries.shape
    taps = filter_taps.shape[0]
    peers = lax.axis_size("ctx")
    direct = peers == DIRECT_PEERS
    scale = 1.0 / math.sqrt(peers * rows)
    chunks = channels // WIDTH
    matrices = [jnp.asarray(m) for m in transforms(2 * rows)]
    lanes = peers // 2 if direct else 2
    share = taps // lanes if direct else 32
    like = jax.ShapeDtypeStruct((rows, channels), BF16)
    hbm = pl.BlockSpec(memory_space=pltpu.HBM)
    tile = (chunks, rows, WIDTH)
    dma = pltpu.SemaphoreType.DMA
    whole = [pltpu.VMEM(x.shape, BF16)
             for x in (queries, key_proj, value_proj, filter_taps, *matrices)]
    results = pl.pallas_call(
        functools.partial(kernel, peers, direct, scale),
        name="hyena_backward",
        out_shape=[like, like, like,
                   jax.ShapeDtypeStruct((taps, channels), BF16 if direct else F32)],
        in_specs=[hbm] * 8,
        out_specs=[hbm] * 4,
        scratch_shapes=[pltpu.VMEM((rows, channels), BF16)] * 3
        + [pltpu.VMEM((taps, channels), BF16 if direct else F32)] + whole + [pltpu.VMEM((rows, channels), BF16)]
        + [pltpu.VMEM(tile, BF16)] * 4 + [
            pltpu.VMEM((chunks, taps, WIDTH), BF16),
            pltpu.VMEM((lanes - 1, chunks, share, WIDTH), BF16),
            pltpu.VMEM((chunks, share // 2, WIDTH), BF16),
            pltpu.VMEM((chunks, share // 2, WIDTH), BF16),
            pltpu.VMEM((chunks, 2 * rows, WIDTH), F32),
            dma((2, chunks)), dma((6,)), dma((2,)), dma((2, chunks)), dma((2, chunks)),
            dma((lanes - 1, chunks)), dma((lanes - 1, chunks)), dma((chunks,)), dma((chunks,)),
            dma((lanes - 1, chunks)), dma((lanes - 1, chunks)),
            dma((lanes, chunks)), dma((lanes, chunks)), dma((4, chunks)),
        ],
        compiler_params=pltpu.CompilerParams(
            collective_id=0, has_side_effects=True, vmem_limit_bytes=VMEM_LIMIT
        ),
        cost_estimate=pl.CostEstimate(
            flops=20 * rows * rows * channels, bytes_accessed=18 * rows * channels,
            transcendentals=0,
        ),
    )(queries, key_proj, value_proj, out_grad, filter_taps, *matrices)
    results = list(results)
    if not direct:
        results[3] = (lax.psum(results[3], "ctx") * scale).astype(BF16)
    return tuple(pl.pallas_call(
        deliver,
        name="deliver",
        out_shape=[jax.ShapeDtypeStruct(x.shape, x.dtype) for x in results],
        in_specs=[hbm] * 4,
        out_specs=[hbm] * 4,
        scratch_shapes=[pltpu.VMEM(x.shape, x.dtype) for x in results] + [dma((2, 4, CUTS))],
        compiler_params=pltpu.CompilerParams(vmem_limit_bytes=VMEM_LIMIT),
    )(*results))


def solution(mesh):
    tokens = P(("grp", "ctx"), "tp")
    return jax.shard_map(
        local,
        mesh=mesh,
        in_specs=(tokens, tokens, tokens, P(("grp", "ctx", "tp"), None), P(None, "tp")),
        out_specs=(tokens, tokens, tokens, P(None, ("grp", "tp"))),
        check_vma=False,
    )
```

time: 62 us -> 49.1 us (0.79)
  the two profiles are of different devices: /device:TPU:24 before, /device:TPU:0 now
where the time goes in v2:
time: 49.1 us; the launch traced here: 49 us
  Pallas kernels  48.3 us (98%)
  between operations  0.64 us (1%)
    pallas_call x1, Pallas kernels, local(): pl.pallas_call(functools.partial(kernel, peers, direct, scale), name='hye...  45.8 us
    pallas_call x1, Pallas kernels, local(): pl.pallas_call(deliver, name='deliver', out_shape=[jax.ShapeDtypeStruct(x...  2.57 us

profile of v2, /device:TPU:0, one launch (start us, length us, event | category | flops | bytes accessed | tf_op | source)
XLA Modules:
  0.0 49.0 jit_solution(12830381407619433320)
XLA Ops:
  0.6 45.8 %hyena_backward.1 = (bf16[128,2048]{1,0:T(8,128)(2,1)}, bf16[128,2048]{1,0:T(8,128)(2,1)}, bf16[128,2048]{1,0:T(8,128)(2,1)}, bf16[128,2048]{1,0:T(8,128)(2,1)}) custom-call(bf16[128,2048]{1,0:T(8,128)(2,1)} %q_hbm.1, bf16[128,2048]{1,0:T(8,128)(2,1)} %k_hbm.1, bf16[128,2048]{1,0:T(8,128)(2,1)} %v_hbm.1, bf16[64,4096]{1,0:T(8,128)(2,1)} %og_hbm.1, ...), custom_call_target="tpu_custom_call" | custom-call | flops 671088640 | bytes 4718592 | tf_op jit(solution)/shard_map/hyena_backward/pallas_call | solution.py:353
  46.4 2.6 %deliver.1 = (bf16[128,2048]{1,0:T(8,128)(2,1)}, bf16[128,2048]{1,0:T(8,128)(2,1)}, bf16[128,2048]{1,0:T(8,128)(2,1)}, bf16[128,2048]{1,0:T(8,128)(2,1)}) custom-call(bf16[128,2048]{1,0:T(8,128)(2,1)} %get-tuple-element.8.refs_0_, bf16[128,2048]{1,0:T(8,128)(2,1)} %get-tuple-element.9.refs_1_, bf16[128,2048]{1,0:T(8,128)(2,1)} %get-tuple-element.10.refs_2_, ...), custom_call_target="tpu_custom_call" | custom-call | tf_op jit(solution)/shard_map/deliver/pallas_call | solution.py:384

commit v3 on v2

--- a/solution.py
+++ b/solution.py
@@ -18,7 +18,8 @@
 VMEM_LIMIT = 60 * 1024 * 1024
 DIRECT_PEERS = 8
 PLAN = (
-    "g0 g1 g2 g3 h0 h1 h2 h3 C0 C1 s0 C2 s1 L0 C3 s2 s3 L1 P0 L2 P1 L3 P2 F0 P3 F1 D0 F2 D1 F3 D2 D3"
+    "g0 g1 g2 g3 C0 h0 h1 C1 s0 M0 h2 h3 C2 s1 M1 L0 X0 C3 s2 s3 "
+    "M2 L1 P0 X1 M3 L2 P1 X2 L3 P2 X3 P3 D0 D1 D2 D3"
 )
 
 
@@ -69,9 +70,9 @@
     q_hbm, k_hbm, v_hbm, og_hbm, h_hbm, fwd_hbm, inv0_hbm, inv1_hbm,
     dq_hbm, dk_hbm, dv_hbm, df_hbm,
     dq_ref, dk_ref, dv_ref, df_ref, q_ref, k_ref, v_ref, h_ref, fwd_ref, inv0_ref, inv1_ref,
-    up, prod, gate, before, after, part, lane_in, pair_in, pair_out, hspec,
+    up, prod, gate, before, after, part, lane_in, pair_in, pair_out, hspec, pspecs,
     kv_sems, in_sems, up_sems, halo_send, halo_recv,
-    lane_send, lane_recv, pair_send, pair_recv, ag_send, ag_recv, fw_send, fw_recv, out_sems,
+    lane_send, lane_recv, pair_send, pair_recv, ag_send, ag_recv, out_sems,
 ):
     grp, me, core = (lax.axis_index(a) for a in ("grp", "ctx", "tp"))
     rows, channels = q_ref.shape
@@ -139,15 +140,18 @@
         )
 
     share = taps // lanes if direct else taps
-    piece = share // 2
+
+    near_lane = place + 1 - 2 * lax.rem(place, 2)
+    far_block = lax.rem(place + 2, lanes)
 
     def scatter(step, index):
-        owner = lax.rem(place + step, lanes)
+        owner = (near_lane, lax.rem(near_lane + 2, lanes), far_block)[step - 1]
+        target = 2 * (near_lane if step < 3 else far_block) + side
         return pltpu.make_async_remote_copy(
             src_ref=part.at[index, pl.ds(pl.multiple_of(owner * share, share), share)],
             dst_ref=lane_in.at[step - 1, index],
             send_sem=lane_send.at[step - 1, index], recv_sem=lane_recv.at[step - 1, index],
-            device_id=at(lane(step)), device_id_type=MESH,
+            device_id=at(target), device_id_type=MESH,
         )
 
     def swap(index):
@@ -159,8 +163,8 @@
 
     def block(step, index):
         holder = lax.rem(place + lanes - step, lanes)
-        start = pl.multiple_of(holder * share + side * piece, piece)
-        return df_ref.at[pl.ds(start, piece), columns(index)]
+        start = pl.multiple_of(holder * share, share)
+        return df_ref.at[pl.ds(start, share), columns(index)]
 
     def collect(step, index):
         return pltpu.make_async_remote_copy(
@@ -169,13 +173,6 @@
             device_id=at(lane(step)), device_id_type=MESH,
         )
 
-    def forward(step, index):
-        return pltpu.make_async_remote_copy(
-            src_ref=block(step, index), dst_ref=block(step, index),
-            send_sem=fw_send.at[step, index], recv_sem=fw_recv.at[step, index],
-            device_id=at(twin), device_id_type=MESH,
-        )
-
     def store(number, index):
         ref = (dq_ref, dk_ref, dv_ref, df_ref)[number]
         hbm = (dq_hbm, dk_hbm, dv_hbm, df_hbm)[number]
@@ -232,12 +229,16 @@
         terms = restore(inv0_ref[...], times_conj(gspec, pspec))
         if direct:
             part[index] = terms.astype(BF16)
-            for step in range(1, lanes):
+            for step in (2, 1):
                 scatter(step, index).start()
         else:
             df_ref[:, cols] = terms
             store(3, index).start()
-        mixture = restore(inv1_ref[...], times(pspec, hspec[index]))
+        pspecs[index] = pspec
+
+    def mix(index):
+        cols = columns(index)
+        mixture = restore(inv1_ref[...], times(pspecs[index], hspec[index]))
         dq_ref[:, cols] = (up[:, cols].astype(F32) * mixture).astype(BF16)
         store(0, index).start()
 
@@ -255,39 +256,39 @@
         store(1, index).start()
         store(2, index).start()
 
-    def lane_total(index, which):
-        start = pl.multiple_of(place * share + which * piece, piece)
-        total = part[index, pl.ds(start, piece)].astype(F32)
-        within = pl.ds(pl.multiple_of(which * piece, piece), piece)
-        for step in range(1, lanes):
-            total = total + lane_in[step - 1, index, within].astype(F32)
+    def lane_total(index):
+        own = pl.ds(pl.multiple_of(place * share, share), share)
+        total = part[index, own].astype(F32)
+        for slot in (0, 2):
+            total = total + lane_in[slot, index].astype(F32)
         return total
 
+    def halve(index):
+        scatter(2, index).wait_recv()
+        other = pl.ds(pl.multiple_of(far_block * share, share), share)
+        total = part[index, other].astype(F32) + lane_in[1, index].astype(F32)
+        part[index, other] = total.astype(BF16)
+        scatter(3, index).start()
+
     def reduce_lane(index):
-        for step in range(1, lanes):
+        for step in (1, 3):
             scatter(step, index).wait_recv()
-        pair_out[index] = lane_total(index, 1 - side).astype(BF16)
+        pair_out[index] = lane_total(index).astype(BF16)
         swap(index).start()
 
     def reduce_pair(index):
         swap(index).wait_recv()
-        total = lane_total(index, side) + pair_in[index].astype(F32)
+        total = pair_out[index].astype(F32) + pair_in[index].astype(F32)
         block(0, index)[...] = (total * scale).astype(BF16)
         for step in range(1, lanes):
             collect(step, index).start()
-        forward(0, index).start()
-
-    def pass_on(index):
-        for step in range(1, lanes):
-            collect(step, index).wait_recv()
-            forward(step, index).start()
 
     def taps_spectrum(index):
         hspec[index] = spectrum(fwd_ref[:, :taps], h_ref[:, columns(index)])
 
-    run = dict(g=make_gate, s=send_gate, h=taps_spectrum, C=first, D=second)
+    run = dict(g=make_gate, s=send_gate, h=taps_spectrum, C=first, X=mix, D=second)
     if direct:
-        run.update(L=reduce_lane, P=reduce_pair, F=pass_on)
+        run.update(M=halve, L=reduce_lane, P=reduce_pair)
     for entry in PLAN.split():
         if entry[0] in run:
             run[entry[0]](int(entry[1]))
@@ -304,10 +305,8 @@
         if direct:
             for step in range(1, lanes):
                 scatter(step, index).wait_send()
-                collect(step, index).wait_send()
+                collect(step, index).wait()
             swap(index).wait_send()
-            for step in range(lanes):
-                forward(step, index).wait()
             store(3, index).start()
     for index in range(chunks):
         for number in range(4):
@@ -362,13 +361,14 @@
         + [pltpu.VMEM(tile, BF16)] * 4 + [
             pltpu.VMEM((chunks, taps, WIDTH), BF16),
             pltpu.VMEM((lanes - 1, chunks, share, WIDTH), BF16),
-            pltpu.VMEM((chunks, share // 2, WIDTH), BF16),
-            pltpu.VMEM((chunks, share // 2, WIDTH), BF16),
+            pltpu.VMEM((chunks, share, WIDTH), BF16),
+            pltpu.VMEM((chunks, share, WIDTH), BF16),
+            pltpu.VMEM((chunks, 2 * rows, WIDTH), F32),
             pltpu.VMEM((chunks, 2 * rows, WIDTH), F32),
             dma((2, chunks)), dma((6,)), dma((2,)), dma((2, chunks)), dma((2, chunks)),
             dma((lanes - 1, chunks)), dma((lanes - 1, chunks)), dma((chunks,)), dma((chunks,)),
             dma((lanes - 1, chunks)), dma((lanes - 1, chunks)),
-            dma((lanes, chunks)), dma((lanes, chunks)), dma((4, chunks)),
+            dma((4, chunks)),
         ],
         compiler_params=pltpu.CompilerParams(
             collective_id=0, has_side_effects=True, vmem_limit_bytes=VMEM_LIMIT

time: 49.1 us -> 48.9 us (level); the launches traced: 49 us -> 48.3 us
  Pallas kernels: 48.3 us -> 47.6 us
    pallas_call x1, Pallas kernels: 45.8 us -> 45.1 us  [local(): pl.pallas_call(functools.partial(kernel, peers, direct, scale), name='hye...]
where the time goes in v3:
time: 48.9 us; the launch traced here: 48.3 us
  Pallas kernels  47.6 us (97%)
  between operations  0.64 us (1%)
    pallas_call x1, Pallas kernels, local(): pl.pallas_call(functools.partial(kernel, peers, direct, scale), name='hye...  45.1 us
    pallas_call x1, Pallas kernels, local(): pl.pallas_call(deliver, name='deliver', out_shape=[jax.ShapeDtypeStruct(x...  2.57 us

profile of v3, /device:TPU:0, one launch (start us, length us, event | category | flops | bytes accessed | tf_op | source)
XLA Modules:
  0.0 48.3 jit_solution(7555317896065823149)
XLA Ops:
  0.6 45.1 %hyena_backward.1 = (bf16[128,2048]{1,0:T(8,128)(2,1)}, bf16[128,2048]{1,0:T(8,128)(2,1)}, bf16[128,2048]{1,0:T(8,128)(2,1)}, bf16[128,2048]{1,0:T(8,128)(2,1)}) custom-call(bf16[128,2048]{1,0:T(8,128)(2,1)} %q_hbm.1, bf16[128,2048]{1,0:T(8,128)(2,1)} %k_hbm.1, bf16[128,2048]{1,0:T(8,128)(2,1)} %v_hbm.1, bf16[64,4096]{1,0:T(8,128)(2,1)} %og_hbm.1, ...), custom_call_target="tpu_custom_call" | custom-call | flops 671088640 | bytes 4718592 | tf_op jit(solution)/shard_map/hyena_backward/pallas_call | solution.py:352
  45.7 2.6 %deliver.1 = (bf16[128,2048]{1,0:T(8,128)(2,1)}, bf16[128,2048]{1,0:T(8,128)(2,1)}, bf16[128,2048]{1,0:T(8,128)(2,1)}, bf16[128,2048]{1,0:T(8,128)(2,1)}) custom-call(bf16[128,2048]{1,0:T(8,128)(2,1)} %get-tuple-element.8.refs_0_, bf16[128,2048]{1,0:T(8,128)(2,1)} %get-tuple-element.9.refs_1_, bf16[128,2048]{1,0:T(8,128)(2,1)} %get-tuple-element.10.refs_2_, ...), custom_call_target="tpu_custom_call" | custom-call | tf_op jit(solution)/shard_map/deliver/pallas_call | solution.py:384
